TPU v7x, 32 devices: a whole 2x2x4 slice. The times are simulated.
32 devices in a mesh: slab: 8 (over z, x), row: 4 (over y, core).
Axes of the slice: x: 2, y: 2, z: 4, core: 2. Of those that a mesh axis runs over, the one named last changes fastest.
Arguments:
- panel: bfloat16 [8, 16, 128, 256], P('slab', 'row'), may hold values from -6 to 6
- blocks: bfloat16 [8, 16, 6, 128, 128], P('slab', 'row'), may hold values from -0.109375 to 0.109375
- offsets: int32 [8, 16, 6], P('slab', 'row'), may hold values from 0 to 8
- stiff_diag: float32 [8, 16, 128], P('slab', 'row'), may hold values from 1 to 3
- base_mass: float32 [8, 16, 128], P('slab', 'row'), may hold values from 1 to 6
- mistune: float32 [16, 128], replicated, may hold values from 0.5 to 1.5
- pattern: int32 [8, 16], P('slab', 'row'), may hold values from 0 to 15
Outputs:
- ritz_basis: float32 [8, 16, 128, 256], P('slab', 'row')
- ritz_matrix: float32 [256, 256], replicated
- stiff_image: float32 [8, 16, 128, 256], P('slab', 'row')
All inputs are finite; a program needn't handle non-finite values.
Results may differ from a plain program's by a relative error of at most 0.0013.
Values may be sent and summed in bfloat16 or wider, within the bound.
A program may use at most 64 MiB of HBM per device.

v0:
```python
import jax
import jax.numpy as jnp
from jax import lax
from jax.sharding import PartitionSpec as P

DEG = 8


highest = lax.Precision.HIGHEST
lower_edge = 2.5
upper_edge = 12.0
anchor_point = 0.0


def with_halo(cells, sides, width, closed):
    for axis, dim in sides:
        count = lax.axis_size(axis)
        ends = count if closed else count - 1
        head = lax.slice_in_dim(cells, 0, width, axis=dim)
        tail = lax.slice_in_dim(cells, cells.shape[dim] - width, cells.shape[dim], axis=dim)
        cells = jnp.concatenate(
            [
                lax.ppermute(tail, axis, [(i, (i + 1) % count) for i in range(ends)]),
                cells,
                lax.ppermute(head, axis, [((i + 1) % count, i) for i in range(ends)]),
            ],
            axis=dim,
        )
    return cells


def filter_scales(degree):
    half_width = (upper_edge - lower_edge) / 2.0
    centre_point = (upper_edge + lower_edge) / 2.0
    first_scale = half_width / (anchor_point - centre_point)
    doubled = 2.0 / first_scale
    scales = [(first_scale / half_width, 0.0)]
    previous = first_scale
    for section in range(1, degree):
        current = 1.0 / (doubled - previous)
        scales.append((2.0 * current / half_width, previous * current))
        previous = current
    return (centre_point, scales)


def neighbour_index(offsets, slab_blocks, cross_blocks):
    slab_pos = jnp.arange(slab_blocks, dtype=jnp.int32)[:, None, None]
    cross_pos = jnp.arange(cross_blocks, dtype=jnp.int32)[None, :, None]
    return ((slab_pos + offsets // 3) * (cross_blocks + 2) + cross_pos + offsets % 3).reshape(-1)


def couple(extended, coupling, flat_index, precision_kind):
    table = extended.reshape((-1,) + extended.shape[2:])
    picked = jnp.take(table, flat_index, axis=0)
    picked = picked.reshape(coupling.shape[:3] + extended.shape[2:])
    return jnp.einsum(
        "ijsab,ijsbv->ijav",
        coupling,
        picked,
        preferred_element_type=jnp.float32,
        precision=precision_kind,
    )


def extend_rounded(rounded):
    widened = with_halo(rounded, (("slab", 0),), 1, True)
    return with_halo(widened, (("row", 1),), 1, False)


def extend_exact(field):
    widened = with_halo(field, (("slab", 0),), 1, True)
    return with_halo(widened, (("row", 1),), 1, False)


def stiff_full(field, wide_blocks, flat_index, stiff_diag):
    extended = extend_exact(field)
    return stiff_diag[..., None] * field + couple(extended, wide_blocks, flat_index, highest)


def shards(panel, blocks, offsets, stiff_diag, base_mass, mistune, pattern):
    slab_blocks, cross_blocks, block_rows, vectors = panel.shape
    total_rows = (
        slab_blocks * cross_blocks * block_rows * lax.axis_size("slab") * lax.axis_size("row")
    )
    levels = mistune.shape[0]
    one_hot = (pattern[:, :, None] == jnp.arange(levels, dtype=jnp.int32)).astype(jnp.float32)
    blade_factor = jnp.einsum("ijp,pb->ijb", one_hot, mistune, precision=highest)
    mass = base_mass * blade_factor
    inv_mass = 1.0 / mass
    flat_index = neighbour_index(offsets, slab_blocks, cross_blocks)
    centre_point, scales = filter_scales(DEG)
    current = panel.astype(jnp.float32)
    previous = jnp.zeros_like(current)
    for section in range(DEG):
        rounded = current.astype(jnp.bfloat16)
        rounded = lax.optimization_barrier(rounded)
        extended = extend_rounded(rounded)
        stiff_term = stiff_diag[..., None] * rounded.astype(jnp.float32) + couple(
            extended, blocks, flat_index, None
        )
        image = inv_mass[..., None] * stiff_term
        gain_factor, carry_factor = scales[section]
        following = gain_factor * (image - centre_point * current) - carry_factor * previous
        previous = current
        current = following
    flat = current.reshape(-1, vectors)
    weighted = (mass[..., None] * current).reshape(-1, vectors)
    local_mass = jnp.einsum("rv,rw->vw", weighted, flat, precision=highest)
    wide_blocks = blocks.astype(jnp.float32)
    identity = jnp.eye(vectors, dtype=jnp.float32)
    mass_gram = lax.psum(local_mass, ("slab", "row")) / total_rows
    lower_tri = jnp.linalg.cholesky(mass_gram)
    back = jax.scipy.linalg.solve_triangular(lower_tri, identity, lower=True).T
    ritz_basis = jnp.dot(flat, back, precision=highest).reshape(current.shape)
    stiff_image = stiff_full(ritz_basis, wide_blocks, flat_index, stiff_diag)
    local_stiff = jnp.einsum(
        "rv,rw->vw",
        ritz_basis.reshape(-1, vectors),
        stiff_image.reshape(-1, vectors),
        precision=highest,
    )
    ritz_matrix = lax.psum(local_stiff, ("slab", "row")) / total_rows
    return (ritz_basis, ritz_matrix, stiff_image)


def solution(mesh):
    return jax.shard_map(
        shards,
        mesh=mesh,
        in_specs=(
            P("slab", "row", None, None),
            P("slab", "row", None, None, None),
            P("slab", "row", None),
            P("slab", "row", None),
            P("slab", "row", None),
            P(),
            P("slab", "row"),
        ),
        out_specs=(P("slab", "row", None, None), P(), P("slab", "row", None, None)),
        check_vma=False,
    )
```

profile of v0, /device:TPU:0, one launch (start us, length us, event | category | flops | bytes accessed | tf_op | source)
XLA Modules:
  0.0 583.0 jit_solution(1588690897605442606)
XLA Ops:
  7.2 6.0 %collective-permute-start.1 = (bf16[1,4,128,256]{3,2,1,0:T(8,128)(2,1)}, bf16[1,4,128,256]{3,2,1,0:T(8,128)(2,1)S(1)}, u32[]{:S(2)}, u32[]{:S(2)}) collective-permute-start(bf16[1,4,128,256]{3,2,1,0:T(8,128)(2,1)} %param.9), channel_id=1, source_target_pairs={{4,0},{8,4},{12,8},{16,12},{20,16},{24,20},{28,24},{0,28},{5,1},{9... | collective-permute-start | bytes 786440 | tf_op jit(solution)/shard_map/ppermute | solution.py:25
  15.5 3.6 collective-permute-done.1
  19.1 4.8 collective-permute-done
  27.5 3.8 collective-permute-done.3
  36.4 3.5 collective-permute-start.5
  39.9 3.9 collective-permute-done.5
  43.8 6.4 %collective-permute-done.4 = bf16[1,4,128,256]{3,2,1,0:T(8,128)(2,1)S(1)} collective-permute-done((bf16[1,4,128,256]{3,2,1,0:T(8,128)(2,1)S(1)}, bf16[1,4,128,256]{3,2,1,0:T(8,128)(2,1)S(1)}, u32[]{:S(2)}, u32[]{:S(2)}) %collective-permute-start.4) | collective-permute-done | bytes 262176 | tf_op jit(solution)/shard_map/ppermute | solution.py:23
  50.3 3.4 collective-permute-start.6
  64.5 4.0 collective-permute-done.9
  68.5 7.3 %collective-permute-done.8 = bf16[1,4,128,256]{3,2,1,0:T(8,128)(2,1)S(1)} collective-permute-done((bf16[1,4,128,256]{3,2,1,0:T(8,128)(2,1)S(1)}, bf16[1,4,128,256]{3,2,1,0:T(8,128)(2,1)S(1)}, u32[]{:S(2)}, u32[]{:S(2)}) %collective-permute-start.8) | collective-permute-done | bytes 262176 | tf_op jit(solution)/shard_map/ppermute | solution.py:23
  89.6 4.3 collective-permute-done.13
  93.9 7.8 %collective-permute-done.12 = bf16[1,4,128,256]{3,2,1,0:T(8,128)(2,1)S(1)} collective-permute-done((bf16[1,4,128,256]{3,2,1,0:T(8,128)(2,1)S(1)}, bf16[1,4,128,256]{3,2,1,0:T(8,128)(2,1)S(1)}, u32[]{:S(2)}, u32[]{:S(2)}) %collective-permute-start.12) | collective-permute-done | bytes 262176 | tf_op jit(solution)/shard_map/ppermute | solution.py:23
  115.1 4.4 collective-permute-done.17
  119.4 7.1 %collective-permute-done.16 = bf16[1,4,128,256]{3,2,1,0:T(8,128)(2,1)S(1)} collective-permute-done((bf16[1,4,128,256]{3,2,1,0:T(8,128)(2,1)S(1)}, bf16[1,4,128,256]{3,2,1,0:T(8,128)(2,1)S(1)}, u32[]{:S(2)}, u32[]{:S(2)}) %collective-permute-start.16) | collective-permute-done | bytes 262176 | tf_op jit(solution)/shard_map/ppermute | solution.py:23
  139.1 3.9 collective-permute-done.21
  143.0 8.0 %collective-permute-done.20 = bf16[1,4,128,256]{3,2,1,0:T(8,128)(2,1)S(1)} collective-permute-done((bf16[1,4,128,256]{3,2,1,0:T(8,128)(2,1)S(1)}, bf16[1,4,128,256]{3,2,1,0:T(8,128)(2,1)S(1)}, u32[]{:S(2)}, u32[]{:S(2)}) %collective-permute-start.20) | collective-permute-done | bytes 262176 | tf_op jit(solution)/shard_map/ppermute | solution.py:23
  159.6 3.3 collective-permute-start.25
  162.9 3.9 collective-permute-done.25
  166.8 8.1 %collective-permute-done.24 = bf16[1,4,128,256]{3,2,1,0:T(8,128)(2,1)S(1)} collective-permute-done((bf16[1,4,128,256]{3,2,1,0:T(8,128)(2,1)S(1)}, bf16[1,4,128,256]{3,2,1,0:T(8,128)(2,1)S(1)}, u32[]{:S(2)}, u32[]{:S(2)}) %collective-permute-start.24) | collective-permute-done | bytes 262176 | tf_op jit(solution)/shard_map/ppermute | solution.py:23
  188.7 3.9 collective-permute-done.29
  192.6 8.2 %collective-permute-done.28 = bf16[1,4,128,256]{3,2,1,0:T(8,128)(2,1)S(1)} collective-permute-done((bf16[1,4,128,256]{3,2,1,0:T(8,128)(2,1)S(1)}, bf16[1,4,128,256]{3,2,1,0:T(8,128)(2,1)S(1)}, u32[]{:S(2)}, u32[]{:S(2)}) %collective-permute-start.28) | collective-permute-done | bytes 262176 | tf_op jit(solution)/shard_map/ppermute | solution.py:23
  213.0 126.5 %all-reduce.4.cloned.1.call-done = f32[256,256]{0,1:T(8,128)} async-done(((f32[256,256]{0,1:T(8,128)}), f32[256,256]{0,1:T(8,128)}) %all-reduce.4.cloned.1.call-update) | async-done | bytes 262160 | tf_op jit(solution)/shard_map/psum | solution.py:111
  341.5 11.7 %cholesky.50 = f32[128,128]{1,0:T(8,128)S(1)} custom-call(f32[128,128]{1,0:T(8,128)S(1)} %cholesky.118), custom_call_target="Cholesky" | custom-call | tf_op jit(solution)/shard_map/jit(cholesky)/cholesky | solution.py:112
  353.3 9.8 %custom-call.15 = f32[1,128,128]{1,2,0:T(8,128)S(1)} custom-call(f32[1,128,128]{2,1,0:T(8,128)S(1)} %get-tuple-element.48), custom_call_target="InvertDiagBlocksLowerTriangular" | custom-call | tf_op jit(solution)/shard_map/jit(cholesky)/cholesky | solution.py:112
  363.6 11.7 %cholesky.105 = f32[128,128]{1,0:T(8,128)S(1)} custom-call(f32[128,128]{1,0:T(8,128)S(1)} %convolution_subtract_fusion.1), custom_call_target="Cholesky" | custom-call | tf_op jit(solution)/shard_map/jit(cholesky)/cholesky | solution.py:112
  377.4 4.2 while.1
  381.6 19.7 %custom-call.16 = f32[2,128,128]{1,2,0:T(8,128)S(1)} custom-call(f32[2,128,128]{2,1,0:T(8,128)S(1)} %get-tuple-element.11), custom_call_target="InvertDiagBlocksLowerTriangular" | custom-call | tf_op jit(solution)/shard_map/jit(_solve_triangular)/triangular_solve | solution.py:113
  406.0 20.9 %collective-permute-done.33 = f32[1,4,128,256]{3,2,1,0:T(8,128)S(1)} collective-permute-done((f32[1,4,128,256]{3,2,1,0:T(8,128)S(1)}, f32[1,4,128,256]{3,2,1,0:T(8,128)S(1)}, u32[]{:S(2)}, u32[]{:S(2)}) %collective-permute-start.33) | collective-permute-done | bytes 524320 | tf_op jit(solution)/shard_map/ppermute | solution.py:25
  431.1 3.3 collective-permute-done.35
  436.0 4.0 gather_fusion
  440.1 3.4 fusion.45
  445.2 129.2 %all-reduce.6.cloned.1.call-done = f32[256,256]{0,1:T(8,128)} async-done(((f32[256,256]{0,1:T(8,128)}), f32[256,256]{0,1:T(8,128)}) %all-reduce.6.cloned.1.call-update) | async-done | bytes 262160 | tf_op jit(solution)/shard_map/psum | solution.py:122
  (172 shorter events, 116.9 us)
Async XLA Ops:
  7.2 332.3 %all-reduce.4.cloned.1.call-start = ((), (), s32[]{:S(2)}) async-start(), calls=%async_computation | async-start | bytes 524288 | tf_op jit(solution)/shard_map/psum | solution.py:111
  7.2 11.9 %collective-permute-start.1 = (bf16[1,4,128,256]{3,2,1,0:T(8,128)(2,1)}, bf16[1,4,128,256]{3,2,1,0:T(8,128)(2,1)S(1)}, u32[]{:S(2)}, u32[]{:S(2)}) collective-permute-start(bf16[1,4,128,256]{3,2,1,0:T(8,128)(2,1)} %param.9), channel_id=1, source_target_pairs={{4,0},{8,4},{12,8},{16,12},{20,16},{24,20},{28,24},{0,28},{5,1},{9... | collective-permute-start | bytes 786440 | tf_op jit(solution)/shard_map/ppermute | solution.py:25
  13.3 10.7 %collective-permute-start = (bf16[1,4,128,256]{3,2,1,0:T(8,128)(2,1)}, bf16[1,4,128,256]{3,2,1,0:T(8,128)(2,1)S(1)}, u32[]{:S(2)}, u32[]{:S(2)}) collective-permute-start(bf16[1,4,128,256]{3,2,1,0:T(8,128)(2,1)} %param.9), channel_id=1, source_target_pairs={{0,4},{4,8},{8,12},{12,16},{16,20},{20,24},{24,28},{28,0},{1,5},{5... | collective-permute-start | bytes 786440 | tf_op jit(solution)/shard_map/ppermute | solution.py:23
  26.2 5.1 collective-permute-start.3
  36.4 7.4 %collective-permute-start.5 = (bf16[1,4,128,256]{3,2,1,0:T(8,128)(2,1)S(1)}, bf16[1,4,128,256]{3,2,1,0:T(8,128)(2,1)S(1)}, u32[]{:S(2)}, u32[]{:S(2)}) collective-permute-start(bf16[1,4,128,256]{3,2,1,0:T(8,128)(2,1)S(1)} %get-tuple-element.49), channel_id=1, source_target_pairs={{4,0},{8,4},{12,8},{16,12},{20,16},{24,20},{28,24},{0,28},{5,1},{9... | collective-permute-start | bytes 786440 | tf_op jit(solution)/shard_map/ppermute | solution.py:25
  39.9 10.3 %collective-permute-start.4 = (bf16[1,4,128,256]{3,2,1,0:T(8,128)(2,1)S(1)}, bf16[1,4,128,256]{3,2,1,0:T(8,128)(2,1)S(1)}, u32[]{:S(2)}, u32[]{:S(2)}) collective-permute-start(bf16[1,4,128,256]{3,2,1,0:T(8,128)(2,1)S(1)} %get-tuple-element.49), channel_id=1, source_target_pairs={{0,4},{4,8},{8,12},{12,16},{16,20},{20,24},{24,28},{28,0},{1,5},{5... | collective-permute-start | bytes 786440 | tf_op jit(solution)/shard_map/ppermute | solution.py:23
  50.3 4.7 collective-permute-start.6
  53.7 4.1 collective-permute-start.7
  62.1 6.4 %collective-permute-start.9 = (bf16[1,4,128,256]{3,2,1,0:T(8,128)(2,1)S(1)}, bf16[1,4,128,256]{3,2,1,0:T(8,128)(2,1)S(1)}, u32[]{:S(2)}, u32[]{:S(2)}) collective-permute-start(bf16[1,4,128,256]{3,2,1,0:T(8,128)(2,1)S(1)} %get-tuple-element.51), channel_id=1, source_target_pairs={{4,0},{8,4},{12,8},{16,12},{20,16},{24,20},{28,24},{0,28},{5,1},{9... | collective-permute-start | bytes 786440 | tf_op jit(solution)/shard_map/ppermute | solution.py:25
  64.5 11.3 %collective-permute-start.8 = (bf16[1,4,128,256]{3,2,1,0:T(8,128)(2,1)S(1)}, bf16[1,4,128,256]{3,2,1,0:T(8,128)(2,1)S(1)}, u32[]{:S(2)}, u32[]{:S(2)}) collective-permute-start(bf16[1,4,128,256]{3,2,1,0:T(8,128)(2,1)S(1)} %get-tuple-element.51), channel_id=1, source_target_pairs={{0,4},{4,8},{8,12},{12,16},{16,20},{20,24},{24,28},{28,0},{1,5},{5... | collective-permute-start | bytes 786440 | tf_op jit(solution)/shard_map/ppermute | solution.py:23
  75.9 4.5 collective-permute-start.10
  79.1 3.4 collective-permute-start.11
  87.6 6.4 %collective-permute-start.13 = (bf16[1,4,128,256]{3,2,1,0:T(8,128)(2,1)S(1)}, bf16[1,4,128,256]{3,2,1,0:T(8,128)(2,1)S(1)}, u32[]{:S(2)}, u32[]{:S(2)}) collective-permute-start(bf16[1,4,128,256]{3,2,1,0:T(8,128)(2,1)S(1)} %get-tuple-element.53), channel_id=1, source_target_pairs={{4,0},{8,4},{12,8},{16,12},{20,16},{24,20},{28,24},{0,28},{5,1},{9... | collective-permute-start | bytes 786440 | tf_op jit(solution)/shard_map/ppermute | solution.py:25
  89.5 12.2 %collective-permute-start.12 = (bf16[1,4,128,256]{3,2,1,0:T(8,128)(2,1)S(1)}, bf16[1,4,128,256]{3,2,1,0:T(8,128)(2,1)S(1)}, u32[]{:S(2)}, u32[]{:S(2)}) collective-permute-start(bf16[1,4,128,256]{3,2,1,0:T(8,128)(2,1)S(1)} %get-tuple-element.53), channel_id=1, source_target_pairs={{0,4},{4,8},{8,12},{12,16},{16,20},{20,24},{24,28},{28,0},{1,5},{5... | collective-permute-start | bytes 786440 | tf_op jit(solution)/shard_map/ppermute | solution.py:23
  101.8 4.1 collective-permute-start.14
  113.0 6.4 %collective-permute-start.17 = (bf16[1,4,128,256]{3,2,1,0:T(8,128)(2,1)S(1)}, bf16[1,4,128,256]{3,2,1,0:T(8,128)(2,1)S(1)}, u32[]{:S(2)}, u32[]{:S(2)}) collective-permute-start(bf16[1,4,128,256]{3,2,1,0:T(8,128)(2,1)S(1)} %get-tuple-element.55), channel_id=1, source_target_pairs={{4,0},{8,4},{12,8},{16,12},{20,16},{24,20},{28,24},{0,28},{5,1},{9... | collective-permute-start | bytes 786440 | tf_op jit(solution)/shard_map/ppermute | solution.py:25
  114.6 12.0 %collective-permute-start.16 = (bf16[1,4,128,256]{3,2,1,0:T(8,128)(2,1)S(1)}, bf16[1,4,128,256]{3,2,1,0:T(8,128)(2,1)S(1)}, u32[]{:S(2)}, u32[]{:S(2)}) collective-permute-start(bf16[1,4,128,256]{3,2,1,0:T(8,128)(2,1)S(1)} %get-tuple-element.55), channel_id=1, source_target_pairs={{0,4},{4,8},{8,12},{12,16},{16,20},{20,24},{24,28},{28,0},{1,5},{5... | collective-permute-start | bytes 786440 | tf_op jit(solution)/shard_map/ppermute | solution.py:23
  126.6 4.3 collective-permute-start.18
  136.5 6.5 %collective-permute-start.21 = (bf16[1,4,128,256]{3,2,1,0:T(8,128)(2,1)S(1)}, bf16[1,4,128,256]{3,2,1,0:T(8,128)(2,1)S(1)}, u32[]{:S(2)}, u32[]{:S(2)}) collective-permute-start(bf16[1,4,128,256]{3,2,1,0:T(8,128)(2,1)S(1)} %get-tuple-element.57), channel_id=1, source_target_pairs={{4,0},{8,4},{12,8},{16,12},{20,16},{24,20},{28,24},{0,28},{5,1},{9... | collective-permute-start | bytes 786440 | tf_op jit(solution)/shard_map/ppermute | solution.py:25
  139.1 11.9 %collective-permute-start.20 = (bf16[1,4,128,256]{3,2,1,0:T(8,128)(2,1)S(1)}, bf16[1,4,128,256]{3,2,1,0:T(8,128)(2,1)S(1)}, u32[]{:S(2)}, u32[]{:S(2)}) collective-permute-start(bf16[1,4,128,256]{3,2,1,0:T(8,128)(2,1)S(1)} %get-tuple-element.57), channel_id=1, source_target_pairs={{0,4},{4,8},{8,12},{12,16},{16,20},{20,24},{24,28},{28,0},{1,5},{5... | collective-permute-start | bytes 786440 | tf_op jit(solution)/shard_map/ppermute | solution.py:23
  151.1 3.8 collective-permute-start.22
  159.6 7.2 %collective-permute-start.25 = (bf16[1,4,128,256]{3,2,1,0:T(8,128)(2,1)S(1)}, bf16[1,4,128,256]{3,2,1,0:T(8,128)(2,1)S(1)}, u32[]{:S(2)}, u32[]{:S(2)}) collective-permute-start(bf16[1,4,128,256]{3,2,1,0:T(8,128)(2,1)S(1)} %get-tuple-element.59), channel_id=1, source_target_pairs={{4,0},{8,4},{12,8},{16,12},{20,16},{24,20},{28,24},{0,28},{5,1},{9... | collective-permute-start | bytes 786440 | tf_op jit(solution)/shard_map/ppermute | solution.py:25
  162.9 12.0 %collective-permute-start.24 = (bf16[1,4,128,256]{3,2,1,0:T(8,128)(2,1)S(1)}, bf16[1,4,128,256]{3,2,1,0:T(8,128)(2,1)S(1)}, u32[]{:S(2)}, u32[]{:S(2)}) collective-permute-start(bf16[1,4,128,256]{3,2,1,0:T(8,128)(2,1)S(1)} %get-tuple-element.59), channel_id=1, source_target_pairs={{0,4},{4,8},{8,12},{12,16},{16,20},{20,24},{24,28},{28,0},{1,5},{5... | collective-permute-start | bytes 786440 | tf_op jit(solution)/shard_map/ppermute | solution.py:23
  175.0 3.5 collective-permute-start.26
  177.3 3.3 collective-permute-start.27
  185.7 7.0 %collective-permute-start.29 = (bf16[1,4,128,256]{3,2,1,0:T(8,128)(2,1)S(1)}, bf16[1,4,128,256]{3,2,1,0:T(8,128)(2,1)S(1)}, u32[]{:S(2)}, u32[]{:S(2)}) collective-permute-start(bf16[1,4,128,256]{3,2,1,0:T(8,128)(2,1)S(1)} %get-tuple-element.61), channel_id=1, source_target_pairs={{4,0},{8,4},{12,8},{16,12},{20,16},{24,20},{28,24},{0,28},{5,1},{9... | collective-permute-start | bytes 786440 | tf_op jit(solution)/shard_map/ppermute | solution.py:25
  188.7 12.1 %collective-permute-start.28 = (bf16[1,4,128,256]{3,2,1,0:T(8,128)(2,1)S(1)}, bf16[1,4,128,256]{3,2,1,0:T(8,128)(2,1)S(1)}, u32[]{:S(2)}, u32[]{:S(2)}) collective-permute-start(bf16[1,4,128,256]{3,2,1,0:T(8,128)(2,1)S(1)} %get-tuple-element.61), channel_id=1, source_target_pairs={{0,4},{4,8},{8,12},{12,16},{16,20},{20,24},{24,28},{28,0},{1,5},{5... | collective-permute-start | bytes 786440 | tf_op jit(solution)/shard_map/ppermute | solution.py:23
  200.9 3.7 collective-permute-start.30
  212.8 361.5 %all-reduce.6.cloned.1.call-start = ((), (), s32[]{:S(2)}) async-start(), calls=%async_computation.1 | async-start | bytes 524288 | tf_op jit(solution)/shard_map/psum | solution.py:122
  402.8 24.2 %collective-permute-start.33 = (f32[1,4,128,256]{3,2,1,0:T(8,128)S(1)}, f32[1,4,128,256]{3,2,1,0:T(8,128)S(1)}, u32[]{:S(2)}, u32[]{:S(2)}) collective-permute-start(f32[1,4,128,256]{3,2,1,0:T(8,128)S(1)} %bitcast.261), channel_id=1, source_target_pairs={{4,0},{8,4},{12,8},{16,12},{20,16},{24,20},{28,24},{0,28},{5,1},{9... | collective-permute-start | bytes 1572872 | tf_op jit(solution)/shard_map/ppermute | solution.py:25
  406.0 20.9 %collective-permute-start.32 = (f32[1,4,128,256]{3,2,1,0:T(8,128)S(1)}, f32[1,4,128,256]{3,2,1,0:T(8,128)S(1)}, u32[]{:S(2)}, u32[]{:S(2)}) collective-permute-start(f32[1,4,128,256]{3,2,1,0:T(8,128)S(1)} %bitcast.262), channel_id=1, source_target_pairs={{0,4},{4,8},{8,12},{12,16},{16,20},{20,24},{24,28},{28,0},{1,5},{5... | collective-permute-start | bytes 1572872 | tf_op jit(solution)/shard_map/ppermute | solution.py:23
  429.6 4.8 collective-permute-start.35
  (25 other events, 308.1 us)
Sparse Core Ops, SparseCore 0:
  213.0 126.4 all-reduce.3
  445.3 129.0 all-reduce.5
where the time goes:
time: 584 us; the launch traced here: 583 us
  waiting for transfers between devices  388 us (66%)
  other arithmetic  74.2 us (13%)
  starting transfers between devices  62.6 us (11%)
  local copies, waits for them, and re-layouts  24.9 us (4%)
  matrix products  16.7 us (3%)
  between operations  16.1 us (3%)
    psum x1, waiting for transfers between devices, shards(): ritz_matrix = lax.psum(local_stiff, ('slab', 'row')) / total_rows  129 us
    psum x1, waiting for transfers between devices, shards(): mass_gram = lax.psum(local_mass, ('slab', 'row')) / total_rows  126 us
    ppermute x18, waiting for transfers between devices, with_halo(): lax.ppermute(head, axis, [((i + 1) % count, i) for i in range(ends)])  74.7 us
    ppermute x18, waiting for transfers between devices, with_halo(): lax.ppermute(tail, axis, [(i, (i + 1) % count) for i in range(ends)])  57.9 us
    ppermute x18, starting transfers between devices, with_halo(): lax.ppermute(head, axis, [((i + 1) % count, i) for i in range(ends)])  39.6 us
    another operation x6, other arithmetic, shards(): lower_tri = jnp.linalg.cholesky(mass_gram)  34 us
    ppermute x18, starting transfers between devices, with_halo(): lax.ppermute(tail, axis, [(i, (i + 1) % count) for i in range(ends)])  22.9 us
    another operation x3, other arithmetic, shards(): back = jax.scipy.linalg.solve_triangular(lower_tri, identity, lower=True).T  19.7 us
  transfers between devices with their start and end apart: 38, of which 29 were waited for; matrix products, arithmetic and copies ran while one was open for 0% of the time, Pallas kernels for 0%

commit v1 on v0

v1 whole, which is shorter than its diff:
```python
import functools

import jax
import jax.numpy as jnp
from jax import lax
from jax.experimental import pallas as pl
from jax.experimental.pallas import tpu as pltpu
from jax.sharding import PartitionSpec as P

DEG = 8
MESH = pl.DeviceIdType.MESH

highest = lax.Precision.HIGHEST
lower_edge = 2.5
upper_edge = 12.0
anchor_point = 0.0


def filter_scales(degree):
    half_width = (upper_edge - lower_edge) / 2.0
    centre_point = (upper_edge + lower_edge) / 2.0
    first_scale = half_width / (anchor_point - centre_point)
    doubled = 2.0 / first_scale
    scales = [(first_scale / half_width, 0.0)]
    previous = first_scale
    for section in range(1, degree):
        current = 1.0 / (doubled - previous)
        scales.append((2.0 * current / half_width, previous * current))
        previous = current
    return (centre_point, scales)


def neighbour_index(offsets, cross_blocks):
    cross_pos = jnp.arange(cross_blocks, dtype=jnp.int32)[None, :, None]
    return ((offsets // 3) * (cross_blocks + 2) + cross_pos + offsets % 3).reshape(-1)


def split3_dot(a, b, dims):
    a_hi = a.astype(jnp.bfloat16)
    b_hi = b.astype(jnp.bfloat16)
    a_lo = (a - a_hi.astype(jnp.float32)).astype(jnp.bfloat16)
    b_lo = (b - b_hi.astype(jnp.float32)).astype(jnp.bfloat16)
    dot = functools.partial(
        lax.dot_general, dimension_numbers=(dims, ((), ())), preferred_element_type=jnp.float32
    )
    return dot(a_hi, b_hi) + (dot(a_hi, b_lo) + dot(a_lo, b_hi))


def filter_kernel(
    slabs, rows, cols, slots, halves, lanes,
    index_ref, panel_ref, blocks_ref, inv_ref, diag_ref, mass_ref,
    y_ref, ky_ref, gram_ref,
    ext00, ext01, ext10, ext11, prev_ref, slab_send, slab_recv, row_send, row_recv,
):
    wide = cols + 2
    first = wide + 1
    ext = ((ext00, ext01), (ext10, ext11))
    s = lax.axis_index("slab")
    r = lax.axis_index("row")
    up = lax.rem(s + 1, slabs)
    down = lax.rem(s + slabs - 1, slabs)
    has_left = r > 0
    has_right = r < rows - 1
    centre, scales = filter_scales(DEG)

    barrier = pltpu.get_barrier_semaphore()
    pl.semaphore_signal(barrier, inc=1, device_id=(up, r), device_id_type=MESH)
    pl.semaphore_signal(barrier, inc=1, device_id=(down, r), device_id_type=MESH)

    @pl.when(has_left)
    def _():
        pl.semaphore_signal(barrier, inc=1, device_id=(s, r - 1), device_id_type=MESH)

    @pl.when(has_right)
    def _():
        pl.semaphore_signal(barrier, inc=1, device_id=(s, r + 1), device_id_type=MESH)

    def slab_copies(t):
        p, h = (t // halves) % 2, t % halves
        buf = ext[p][h]
        own = buf.at[pl.ds(first, cols)]
        return [
            pltpu.make_async_remote_copy(
                src_ref=own, dst_ref=buf.at[pl.ds(1 + 2 * wide * lower, cols)],
                send_sem=slab_send.at[p, h, lower], recv_sem=slab_recv.at[p, h, lower],
                device_id=(target, r), device_id_type=MESH,
            )
            for lower, target in ((0, up), (1, down))
        ]

    def row_copies(t, side):
        p, h = (t // halves) % 2, t % halves
        buf = ext[p][h]
        source, place, target = ((cols, 0, r + 1), (1, cols + 1, r - 1))[side]
        return [
            pltpu.make_async_remote_copy(
                src_ref=buf.at[pl.ds(source + wide * k, 1)], dst_ref=buf.at[pl.ds(place + wide * k, 1)],
                send_sem=row_send.at[p, h, side, k], recv_sem=row_recv.at[p, h, side, k],
                device_id=(s, target), device_id_type=MESH,
            )
            for k in range(3)
        ]

    def start_slab(t):
        for copy in slab_copies(t):
            copy.start()

    def wait_slab(t):
        for copy in slab_copies(t):
            copy.wait()

    def start_row(t):
        for side, there in ((0, has_right), (1, has_left)):
            @pl.when(there)
            def _():
                for copy in row_copies(t, side):
                    copy.start()

    def wait_row(t):
        for side, there in ((0, has_right), (1, has_left)):
            @pl.when(there)
            def _():
                for copy in row_copies(t, side):
                    copy.wait_send()
                for copy in row_copies(t, 1 - side):
                    copy.wait_recv()

    def compute(t):
        k, h = t // halves, t % halves
        buf = ext[k % 2][h]
        nxt = ext[(k + 1) % 2][h]
        span = pl.ds(h * lanes, lanes)

        def one(c, carry):
            acc = diag_ref[c] * buf[first + c].astype(jnp.float32) if k < DEG else diag_ref[c] * y_ref[c, :, span]
            for slot in range(slots):
                acc += jnp.dot(
                    blocks_ref[c, slot], buf[index_ref[c * slots + slot]], preferred_element_type=jnp.float32
                )
            if k < DEG:
                gain, back = scales[k]
                cur = y_ref[c, :, span]
                new = gain * (inv_ref[c] * acc - centre * cur)
                if k > 0:
                    new -= back * prev_ref[c, :, span]
                prev_ref[c, :, span] = cur
                y_ref[c, :, span] = new
                nxt[first + c] = new.astype(jnp.bfloat16)
            else:
                ky_ref[c, :, span] = acc
            return carry

        lax.fori_loop(0, cols, one, 0)

    for p in range(2):
        for h in range(halves):
            @pl.when(jnp.logical_not(has_left))
            def _():
                for k in range(3):
                    ext[p][h][wide * k] = jnp.zeros(ext00.shape[1:], jnp.bfloat16)

            @pl.when(jnp.logical_not(has_right))
            def _():
                for k in range(3):
                    ext[p][h][wide * k + cols + 1] = jnp.zeros(ext00.shape[1:], jnp.bfloat16)

    for h in range(halves):
        for c in range(cols):
            ext[0][h][first + c] = panel_ref[c, :, h * lanes:(h + 1) * lanes]

    pl.semaphore_wait(barrier, 2 + (r + rows - 1) // rows + (2 * rows - 2 - r) // rows)

    for h in range(halves):
        start_slab(h)
    y_ref[...] = panel_ref[...].astype(jnp.float32)
    total = halves * (DEG + 1)
    vectors = y_ref.shape[-1]
    depth = cols * y_ref.shape[1]
    for t in range(total + 1):
        if t >= 1:
            wait_row(t - 1)
            compute(t - 1)
            if halves <= t - 1 + halves < total:
                start_slab(t - 1 + halves)
            if t - 1 == halves * DEG - 1:
                flat = y_ref[...].reshape(depth, vectors)
                weight = mass_ref[...].reshape(depth, lanes)
                weighted = jnp.concatenate([weight] * halves, axis=1) * flat
                gram_ref[:vectors] = split3_dot(weighted, flat, ((0,), (0,)))
        if t < total:
            wait_slab(t)
            start_row(t)
    gram_ref[vectors:] = split3_dot(
        y_ref[...].reshape(depth, vectors), ky_ref[...].reshape(depth, vectors), ((0,), (0,))
    )


def sum_kernel(slabs, rows, g_ref, out_ref, first, parts, total, pair_send, pair_recv, a_send, a_recv, b_send, b_recv):
    half = g_ref.shape[0] // 2
    group = slabs * (rows // 2)
    chunk = half // group
    s = lax.axis_index("slab")
    r = lax.axis_index("row")
    core = lax.rem(r, 2)
    me = s * (rows // 2) + r // 2
    partner = (s, r + 1 - 2 * core)

    def member(d):
        q = lax.rem(me + d, group)
        return (q // (rows // 2), lax.rem(q, rows // 2) * 2 + core)

    barrier = pltpu.get_barrier_semaphore()
    pl.semaphore_signal(barrier, inc=1, device_id=partner, device_id_type=MESH)
    for d in range(1, group):
        pl.semaphore_signal(barrier, inc=1, device_id=member(d), device_id_type=MESH)
    pl.semaphore_wait(barrier, group)

    mine = pl.ds(pl.multiple_of(core * half, half), half)
    theirs = pl.ds(pl.multiple_of((1 - core) * half, half), half)
    swap = pltpu.make_async_remote_copy(
        src_ref=g_ref.at[theirs], dst_ref=first, send_sem=pair_send.at[0], recv_sem=pair_recv.at[0],
        device_id=partner, device_id_type=MESH,
    )
    swap.start()
    swap.wait()
    first[...] += g_ref[mine]
    copies = []
    for d in range(1, group):
        q = lax.rem(me + d, group)
        copy = pltpu.make_async_remote_copy(
            src_ref=first.at[pl.ds(pl.multiple_of(q * chunk, chunk), chunk)], dst_ref=parts.at[d],
            send_sem=a_send.at[d], recv_sem=a_recv.at[d], device_id=member(d), device_id_type=MESH,
        )
        copy.start()
        copies.append(copy)
    acc = first[pl.ds(pl.multiple_of(me * chunk, chunk), chunk)]
    for d, copy in enumerate(copies, 1):
        copy.wait()
        acc += parts[d]
    spot = pl.ds(pl.multiple_of(core * half + me * chunk, chunk), chunk)
    total[spot] = acc
    copies = []
    for d in range(1, group):
        copy = pltpu.make_async_remote_copy(
            src_ref=total.at[spot], dst_ref=total.at[spot],
            send_sem=b_send.at[d], recv_sem=b_recv.at[d], device_id=member(d), device_id_type=MESH,
        )
        copy.start()
        copies.append(copy)
    for copy in copies:
        copy.wait()
    swap = pltpu.make_async_remote_copy(
        src_ref=total.at[mine], dst_ref=total.at[mine], send_sem=pair_send.at[1], recv_sem=pair_recv.at[1],
        device_id=partner, device_id_type=MESH,
    )
    swap.start()
    swap.wait()
    out_ref[...] = total[...]


def sum_everywhere(grams, slabs, rows):
    height, width = grams.shape
    group = slabs * rows // 2
    if rows % 2 or height % (2 * group) or (height // (2 * group)) % 8:
        return lax.psum(grams, ("slab", "row"))
    half = height // 2
    vmem = pl.BlockSpec(memory_space=pltpu.VMEM)
    return pl.pallas_call(
        functools.partial(sum_kernel, slabs, rows),
        out_shape=jax.ShapeDtypeStruct(grams.shape, jnp.float32),
        in_specs=[vmem],
        out_specs=vmem,
        scratch_shapes=[
            pltpu.VMEM((half, width), jnp.float32),
            pltpu.VMEM((group, half // group, width), jnp.float32),
            pltpu.VMEM((height, width), jnp.float32),
            pltpu.SemaphoreType.DMA((2,)),
            pltpu.SemaphoreType.DMA((2,)),
            pltpu.SemaphoreType.DMA((group,)),
            pltpu.SemaphoreType.DMA((group,)),
            pltpu.SemaphoreType.DMA((group,)),
            pltpu.SemaphoreType.DMA((group,)),
        ],
        compiler_params=pltpu.CompilerParams(
            collective_id=1, has_side_effects=True, vmem_limit_bytes=16 * 1024 * 1024
        ),
        name="sum_everywhere",
    )(grams)


def shards(slabs, rows, panel, blocks, offsets, stiff_diag, base_mass, mistune, pattern):
    _, cols, block_rows, vectors = panel.shape
    slots = blocks.shape[2]
    total_rows = cols * block_rows * slabs * rows
    levels = mistune.shape[0]
    one_hot = (pattern[:, :, None] == jnp.arange(levels, dtype=jnp.int32)).astype(jnp.float32)
    blade_factor = jnp.einsum("ijp,pb->ijb", one_hot, mistune, precision=highest)
    mass = (base_mass * blade_factor)[0]
    halves = 2
    lanes = vectors // halves
    spread = lambda a: jnp.broadcast_to(a[..., None], (cols, block_rows, lanes))
    vmem = pl.BlockSpec(memory_space=pltpu.VMEM)
    field = jax.ShapeDtypeStruct((cols, block_rows, vectors), jnp.float32)
    cells = 3 * (cols + 2)
    y, ky, grams = pl.pallas_call(
        functools.partial(filter_kernel, slabs, rows, cols, slots, halves, lanes),
        out_shape=(field, field, jax.ShapeDtypeStruct((2 * vectors, vectors), jnp.float32)),
        in_specs=[pl.BlockSpec(memory_space=pltpu.SMEM)] + [vmem] * 5,
        out_specs=(vmem, vmem, vmem),
        scratch_shapes=[pltpu.VMEM((cells, block_rows, lanes), jnp.bfloat16)] * 4
        + [
            pltpu.VMEM((cols, block_rows, vectors), jnp.float32),
            pltpu.SemaphoreType.DMA((2, halves, 2)),
            pltpu.SemaphoreType.DMA((2, halves, 2)),
            pltpu.SemaphoreType.DMA((2, halves, 2, 3)),
            pltpu.SemaphoreType.DMA((2, halves, 2, 3)),
        ],
        compiler_params=pltpu.CompilerParams(
            collective_id=0, has_side_effects=True, vmem_limit_bytes=32 * 1024 * 1024
        ),
        name="filter_and_grams",
    )(neighbour_index(offsets, cols), panel[0], blocks[0], spread(1.0 / mass), spread(stiff_diag[0]), spread(mass))
    grams = sum_everywhere(grams, slabs, rows) / total_rows
    mass_gram, stiff_gram = grams[:vectors], grams[vectors:]
    lower_tri = jnp.linalg.cholesky(mass_gram)
    identity = jnp.eye(vectors, dtype=jnp.float32)
    back = jax.scipy.linalg.solve_triangular(lower_tri, identity, lower=True).T
    flat = y.reshape(-1, vectors)
    ritz_basis = jnp.dot(flat, back, precision=highest).reshape((1,) + y.shape)
    stiff_image = jnp.dot(ky.reshape(-1, vectors), back, precision=highest).reshape((1,) + y.shape)
    ritz_matrix = jnp.dot(back.T, jnp.dot(stiff_gram, back, precision=highest), precision=highest)
    return (ritz_basis, ritz_matrix, stiff_image)


def solution(mesh):
    return jax.shard_map(
        functools.partial(shards, mesh.shape["slab"], mesh.shape["row"]),
        mesh=mesh,
        in_specs=(
            P("slab", "row", None, None),
            P("slab", "row", None, None, None),
            P("slab", "row", None),
            P("slab", "row", None),
            P("slab", "row", None),
            P(),
            P("slab", "row"),
        ),
        out_specs=(P("slab", "row", None, None), P(), P("slab", "row", None, None)),
        check_vma=False,
    )
```

time: 584 us -> 219 us (0.38)
  waiting for transfers between devices: 388 us -> 0 us
  Pallas kernels: 0 us -> 148 us
  starting transfers between devices: 62.6 us -> 0 us
  other arithmetic: 74.2 us -> 54 us
  local copies, waits for them, and re-layouts: 24.9 us -> 7.19 us
  between operations: 16.1 us -> 2.17 us
  matrix products: 16.7 us -> 6.67 us
    psum x2 -> x0, waiting for transfers between devices: 256 us -> none  [the longest x1 129 us: shards(): ritz_matrix = lax.psum(local_stiff, ('slab', 'row')) / total_rows]
    pallas_call x0 -> x2, Pallas kernels: none -> 148 us  [the longest x1 121 us: shards(): pl.pallas_call(functools.partial(filter_kernel, slabs, rows, cols, slots,...]
    ppermute x36 -> x0, waiting for transfers between devices: 133 us -> none  [the longest x18 74.7 us: with_halo(): lax.ppermute(head, axis, [((i + 1) % count, i) for i in range(ends)])]
    ppermute x36 -> x0, starting transfers between devices: 62.5 us -> none  [the longest x18 39.6 us: with_halo(): lax.ppermute(head, axis, [((i + 1) % count, i) for i in range(ends)])]
    gather x9 -> x0, local copies, waits for them, and re-layouts: 17.5 us -> none  [couple(): picked = jnp.take(table, flat_index, axis=0)]
    select_n x10 -> x0, other arithmetic: 10.3 us -> none  [couple(): picked = jnp.take(table, flat_index, axis=0)]
    dot_general x12 -> x4, matrix products: 14.5 us -> 4.5 us  [the longest x1 1.41 us: shards(): jnp.dot(ky.reshape(-1, vectors), back, precision=highest)]
  transfers between devices with their start and end apart: 38 -> 0, of which waited for: 29 -> 0; matrix products, arithmetic and copies ran while one was open for 0% -> 0% of each run, Pallas kernels for 0% -> 0%
where the time goes in v1:
time: 219 us; the launch traced here: 218 us
  Pallas kernels  148 us (68%)
  other arithmetic  54 us (25%)
  local copies, waits for them, and re-layouts  7.19 us (3%)
  matrix products  6.67 us (3%)
    pallas_call x1, Pallas kernels, shards(): pl.pallas_call(functools.partial(filter_kernel, slabs, rows, cols, slots,...  121 us
    another operation x6, other arithmetic, shards(): lower_tri = jnp.linalg.cholesky(mass_gram)  34 us
    pallas_call x1, Pallas kernels, sum_everywhere(): pl.pallas_call(functools.partial(sum_kernel, slabs, rows), out_shape=jax....  27 us
    another operation x3, other arithmetic, shards(): back = jax.scipy.linalg.solve_triangular(lower_tri, identity, lower=True).T  19.9 us

profile of v1, /device:TPU:0, one launch (start us, length us, event | category | flops | bytes accessed | tf_op | source)
XLA Modules:
  0.0 218.4 jit_solution(18018137349595600443)
XLA Ops:
  0.6 0.0 copy-start
  0.7 0.7 copy-done
  1.3 0.9 broadcast_divide_fusion
  2.2 0.1 broadcast_in_dim.12.mass_ref
  2.3 0.1 broadcast_in_dim.9.inv_ref
  2.5 0.8 broadcast_in_dim.11.diag_ref
  3.3 0.1 reshape.69.index_ref
  3.4 1.0 copy-done.2
  4.4 121.2 %filter_and_grams.1 = (f32[4,128,256]{2,1,0:T(8,128)S(1)}, f32[4,128,256]{2,1,0:T(8,128)S(1)}, f32[512,256]{1,0:T(8,128)S(1)}) custom-call(s32[24]{0:T(128)S(1)} %reshape.69.index_ref, bf16[4,128,256]{2,1,0:T(8,128)(2,1)S(1)} %bitcast.57, bf16[4,6,128,128]{3,2,1,0:T(8,128)(2,1)S(1)} %bitcast.56, f32[4,128,128]{2,1,0:T(8,128)S(1)} %broadcast_in_dim.9.inv_ref, ...), custom_call_target="tpu_custom_call" | custom-call | tf_op jit(solution)/shard_map/filter_and_grams/pallas_call | solution.py:305
  125.6 27.0 %sum_everywhere.1 = f32[512,256]{1,0:T(8,128)S(1)} custom-call(f32[512,256]{1,0:T(8,128)S(1)} %get-tuple-element.7.g_ref), custom_call_target="tpu_custom_call" | custom-call | tf_op jit(solution)/shard_map/sum_everywhere/pallas_call | solution.py:268
  152.7 0.2 copy.10
  153.0 0.1 copy.11
  153.2 11.7 %cholesky.50 = f32[128,128]{1,0:T(8,128)S(1)} custom-call(f32[128,128]{1,0:T(8,128)S(1)} %cholesky.118), custom_call_target="Cholesky" | custom-call | tf_op jit(solution)/shard_map/jit(cholesky)/cholesky | solution.py:325
  164.9 9.8 %custom-call.15 = f32[1,128,128]{1,2,0:T(8,128)S(1)} custom-call(f32[1,128,128]{2,1,0:T(8,128)S(1)} %get-tuple-element.30), custom_call_target="InvertDiagBlocksLowerTriangular" | custom-call | tf_op jit(solution)/shard_map/jit(cholesky)/cholesky | solution.py:325
  174.8 0.2 constant_dynamic-update-slice_fusion.1
  175.0 0.3 convolution_subtract_fusion.1
  175.2 11.7 %cholesky.105 = f32[128,128]{1,0:T(8,128)S(1)} custom-call(f32[128,128]{1,0:T(8,128)S(1)} %convolution_subtract_fusion.1), custom_call_target="Cholesky" | custom-call | tf_op jit(solution)/shard_map/jit(cholesky)/cholesky | solution.py:325
  187.0 0.6 compare_reduce_fusion
  189.0 0.1 triangular_solve.63
  189.1 4.0 %while.1 = (s32[]{:T(128)}, f32[256,256]{1,0:T(8,128)S(1)}, s32[2,2]{1,0:T(2,128)S(1)}, f32[2,128,128]{2,1,0:T(8,128)S(1)}, s32[]{:T(128)}) while((s32[]{:T(128)}, f32[256,256]{1,0:T(8,128)S(1)}, s32[2,2]{1,0:T(2,128)S(1)}, f32[2,128,128]{2,1,0:T(8,128)S(1)}, s32[]{:T(128)}) %tuple.28), condition=%wide.while_cond, body=%wide.while_body.sunk | while | flops 2 | bytes 131181 | solution.py:327
  189.1 0.6 fusion.32
  189.7 1.4 bitcast_dynamic-update-slice_fusion.2
  191.1 0.6 fusion.32
  191.7 1.4 bitcast_dynamic-update-slice_fusion.2
  193.1 19.9 %custom-call.16 = f32[2,128,128]{1,2,0:T(8,128)S(1)} custom-call(f32[2,128,128]{2,1,0:T(8,128)S(1)} %get-tuple-element.16), custom_call_target="InvertDiagBlocksLowerTriangular" | custom-call | tf_op jit(solution)/shard_map/jit(_solve_triangular)/triangular_solve | solution.py:327
  213.0 0.3 fusion.7
  213.3 0.3 convolution_subtract_fusion
  213.5 0.3 fusion.11
  213.9 1.4 convolution_bitcast_fusion
  215.3 0.6 fusion.2
  215.9 1.1 fusion.9
  216.9 1.4 convolution_bitcast_fusion.1
  (21 shorter events, 0.3 us)
Async XLA Ops:
  0.6 0.7 copy-start
  0.6 0.7 copy-start.4
  0.7 2.8 %copy-start.1 = (bf16[1,4,6,128,128]{4,3,2,1,0:T(8,128)(2,1)S(1)}, bf16[1,4,6,128,128]{4,3,2,1,0:T(8,128)(2,1)}, u32[]{:S(2)}) copy-start(bf16[1,4,6,128,128]{4,3,2,1,0:T(8,128)(2,1)} %param.8) | copy-start | bytes 2359300
  2.5 0.8 copy-start.3
  3.4 1.0 copy-start.2

commit v2 on v1

--- a/solution.py
+++ b/solution.py
@@ -286,6 +286,69 @@
         ),
         name="sum_everywhere",
     )(grams)
+
+
+def ritz_kernel(total_rows, gram_ref, y_ref, ky_ref, basis_ref, matrix_ref, image_ref, scaled, resid, factor):
+    n = scaled.shape[0]
+    row_id = lax.broadcasted_iota(jnp.int32, (n, n), 0)
+    col_id = lax.broadcasted_iota(jnp.int32, (n, n), 1)
+    unit = (row_id == col_id).astype(jnp.float32)
+    gram = gram_ref[:n] * (1.0 / total_rows)
+    on_diag = gram * unit
+    down = 1.0 / jnp.sqrt(jnp.sum(on_diag, axis=1, keepdims=True))
+    across = 1.0 / jnp.sqrt(jnp.sum(on_diag, axis=0, keepdims=True))
+    scaled[...] = gram * down * across
+    factor[...] = unit
+    resid[...] = scaled[...] - unit
+
+    def distance():
+        return jnp.sum(resid[...] * resid[...])
+
+    def improve():
+        lower = jnp.where(row_id > col_id, resid[...], 0.0) + 0.5 * unit * resid[...]
+        factor[...] = factor[...] - split3_dot(lower, factor[...], ((1,), (0,)))
+
+    def step(state):
+        improve()
+        left = split3_dot(factor[...], scaled[...], ((1,), (0,)))
+        resid[...] = split3_dot(left, factor[...], ((1,), (1,))) - unit
+        return state[0] + 1, distance()
+
+    _, left_over = lax.while_loop(
+        lambda state: jnp.logical_and(state[0] < 8, state[1] > 1e-4), step, (jnp.int32(0), distance())
+    )
+    near = left_over <= 1e-4
+
+    @pl.when(near)
+    def _():
+        improve()
+
+    @pl.when(jnp.logical_not(near))
+    def _():
+        factor[...] = unit
+        resid[...] = scaled[...]
+
+        def eliminate(j, carry):
+            row = resid[pl.ds(j, 1), :]
+            lane = lax.broadcasted_iota(jnp.int32, (1, n), 1)
+            pivot = jnp.sum(jnp.where(lane == j, row, 0.0), axis=1, keepdims=True)
+            column = jnp.sum(jnp.where(col_id == j, resid[...], 0.0), axis=1, keepdims=True)
+            place = lax.broadcasted_iota(jnp.int32, (n, 1), 0)
+            ratio = jnp.where(place > j, column / pivot, 0.0)
+            resid[...] = resid[...] - ratio * row
+            mine = factor[pl.ds(j, 1), :]
+            factor[...] = factor[...] - ratio * mine
+            factor[pl.ds(j, 1), :] = mine / jnp.sqrt(pivot)
+            return carry
+
+        lax.fori_loop(0, n, eliminate, 0)
+
+    inverse = factor[...] * across
+    rows = y_ref.shape[0] * y_ref.shape[1]
+    basis_ref[...] = split3_dot(y_ref[...].reshape(rows, n), inverse, ((1,), (1,))).reshape(basis_ref.shape)
+    image_ref[...] = split3_dot(ky_ref[...].reshape(rows, n), inverse, ((1,), (1,))).reshape(image_ref.shape)
+    left = split3_dot(inverse, gram_ref[n:] * (1.0 / total_rows), ((1,), (0,)))
+    matrix_ref[...] = split3_dot(left, inverse, ((1,), (1,)))
 
 
 def shards(slabs, rows, panel, blocks, offsets, stiff_diag, base_mass, mistune, pattern):
@@ -320,15 +383,18 @@
         ),
         name="filter_and_grams",
     )(neighbour_index(offsets, cols), panel[0], blocks[0], spread(1.0 / mass), spread(stiff_diag[0]), spread(mass))
-    grams = sum_everywhere(grams, slabs, rows) / total_rows
-    mass_gram, stiff_gram = grams[:vectors], grams[vectors:]
-    lower_tri = jnp.linalg.cholesky(mass_gram)
-    identity = jnp.eye(vectors, dtype=jnp.float32)
-    back = jax.scipy.linalg.solve_triangular(lower_tri, identity, lower=True).T
-    flat = y.reshape(-1, vectors)
-    ritz_basis = jnp.dot(flat, back, precision=highest).reshape((1,) + y.shape)
-    stiff_image = jnp.dot(ky.reshape(-1, vectors), back, precision=highest).reshape((1,) + y.shape)
-    ritz_matrix = jnp.dot(back.T, jnp.dot(stiff_gram, back, precision=highest), precision=highest)
+    grams = sum_everywhere(grams, slabs, rows)
+    square = jax.ShapeDtypeStruct((vectors, vectors), jnp.float32)
+    ritz_basis, ritz_matrix, stiff_image = pl.pallas_call(
+        functools.partial(ritz_kernel, total_rows),
+        out_shape=(field, square, field),
+        in_specs=[vmem] * 3,
+        out_specs=(vmem,) * 3,
+        scratch_shapes=[pltpu.VMEM((vectors, vectors), jnp.float32)] * 3,
+        compiler_params=pltpu.CompilerParams(vmem_limit_bytes=32 * 1024 * 1024),
+        name="ritz",
+    )(grams, y, ky)
+    ritz_basis, stiff_image = ritz_basis[None], stiff_image[None]
     return (ritz_basis, ritz_matrix, stiff_image)
 
 

time: 219 us -> 196 us (0.89)
  other arithmetic: 54 us -> 0.77 us
  Pallas kernels: 148 us -> 191 us
  matrix products: 6.67 us -> 0.88 us
  local copies, waits for them, and re-layouts: 7.19 us -> 2.12 us
    another operation x9 -> x0, other arithmetic: 53.9 us -> none  [the longest x6 34 us: shards(): lower_tri = jnp.linalg.cholesky(mass_gram)]
    pallas_call x0 -> x1, Pallas kernels: none -> 43.1 us  [shards(): pl.pallas_call(functools.partial(ritz_kernel, total_rows), out_shape=(fie...]
    dot_general x4 -> x0, matrix products: 4.5 us -> none  [the longest x1 1.41 us: shards(): jnp.dot(ky.reshape(-1, vectors), back, precision=highest)]
    another operation x9 -> x0, local copies, waits for them, and re-layouts: 4.05 us -> none
where the time goes in v2:
time: 196 us
  Pallas kernels  191 us (97%)
  local copies, waits for them, and re-layouts  2.12 us (1%)
    pallas_call x1, Pallas kernels, shards(): pl.pallas_call(functools.partial(filter_kernel, slabs, rows, cols, slots,...  121 us
    pallas_call x1, Pallas kernels, shards(): pl.pallas_call(functools.partial(ritz_kernel, total_rows), out_shape=(fie...  43.1 us
    pallas_call x1, Pallas kernels, sum_everywhere(): pl.pallas_call(functools.partial(sum_kernel, slabs, rows), out_shape=jax....  27.1 us

profile of v2, /device:TPU:0, one launch (start us, length us, event | category | flops | bytes accessed | tf_op | source)
XLA Modules:
  0.0 195.7 jit_solution(3064082901892374845)
XLA Ops:
  0.6 0.0 copy-start
  0.6 0.0 copy-start.1
  0.7 0.8 fusion.2
  1.4 0.1 reshape.36.index_ref
  1.5 0.0 copy-done
  1.5 0.9 broadcast_divide_fusion
  2.4 0.1 broadcast_in_dim.12.inv_ref
  2.5 0.1 broadcast_in_dim.30.mass_ref
  2.7 0.8 broadcast_in_dim.14.diag_ref
  3.5 0.0 copy-done.1
  3.5 0.0 copy-start.2
  3.5 0.9 copy-done.2
  4.5 121.1 %filter_and_grams.1 = (f32[4,128,256]{2,1,0:T(8,128)S(1)}, f32[4,128,256]{2,1,0:T(8,128)S(1)}, f32[512,256]{1,0:T(8,128)S(1)}) custom-call(s32[24]{0:T(128)S(1)} %reshape.36.index_ref, bf16[4,128,256]{2,1,0:T(8,128)(2,1)S(1)} %bitcast.16, bf16[4,6,128,128]{3,2,1,0:T(8,128)(2,1)S(1)} %bitcast.15, f32[4,128,128]{2,1,0:T(8,128)S(1)} %broadcast_in_dim.12.inv_ref, ...), custom_call_target="tpu_custom_call" | custom-call | tf_op jit(solution)/shard_map/filter_and_grams/pallas_call | solution.py:368
  125.5 27.1 %sum_everywhere.1.gram_ref = f32[512,256]{1,0:T(8,128)S(1)} custom-call(f32[512,256]{1,0:T(8,128)S(1)} %get-tuple-element.9.g_ref), custom_call_target="tpu_custom_call" | custom-call | tf_op jit(solution)/shard_map/sum_everywhere/pallas_call | solution.py:268
  152.6 43.1 %ritz.1 = (f32[4,128,256]{2,1,0:T(8,128)}, f32[256,256]{1,0:T(8,128)}, f32[4,128,256]{2,1,0:T(8,128)}) custom-call(f32[512,256]{1,0:T(8,128)S(1)} %sum_everywhere.1.gram_ref, f32[4,128,256]{2,1,0:T(8,128)S(1)} %get-tuple-element.10.y_ref, f32[4,128,256]{2,1,0:T(8,128)S(1)} %get-tuple-element.11.ky_ref), custom_call_target="tpu_custom_call" | custom-call | tf_op jit(solution)/shard_map/ritz/pallas_call | solution.py:388
Async XLA Ops:
  0.6 0.9 copy-start
  0.6 2.9 %copy-start.1 = (bf16[1,4,6,128,128]{4,3,2,1,0:T(8,128)(2,1)S(1)}, bf16[1,4,6,128,128]{4,3,2,1,0:T(8,128)(2,1)}, u32[]{:S(2)}) copy-start(bf16[1,4,6,128,128]{4,3,2,1,0:T(8,128)(2,1)} %param.8) | copy-start | bytes 2359300
  3.5 1.0 copy-start.2

commit v3 on v2

--- a/solution.py
+++ b/solution.py
@@ -47,10 +47,11 @@
 
 
 def filter_kernel(
-    slabs, rows, cols, slots, halves, lanes,
+    slabs, rows, cols, slots, halves, lanes, fused,
     index_ref, panel_ref, blocks_ref, inv_ref, diag_ref, mass_ref,
     y_ref, ky_ref, gram_ref,
     ext00, ext01, ext10, ext11, prev_ref, slab_send, slab_recv, row_send, row_recv,
+    *sum_refs,
 ):
     wide = cols + 2
     first = wide + 1
@@ -63,17 +64,100 @@
     has_right = r < rows - 1
     centre, scales = filter_scales(DEG)
 
+    vectors = y_ref.shape[-1]
+    core = lax.rem(r, 2)
+    group = slabs * (rows // 2)
+    me = s * (rows // 2) + r // 2
+    partner = (s, r + 1 - 2 * core)
+
+    def member(d):
+        q = lax.rem(me + d, group)
+        return (q // (rows // 2), lax.rem(q, rows // 2) * 2 + core)
+
     barrier = pltpu.get_barrier_semaphore()
-    pl.semaphore_signal(barrier, inc=1, device_id=(up, r), device_id_type=MESH)
-    pl.semaphore_signal(barrier, inc=1, device_id=(down, r), device_id_type=MESH)
-
-    @pl.when(has_left)
+    if fused:
+        greet_left = jnp.logical_and(has_left, core == 0)
+        greet_right = jnp.logical_and(has_right, core == 1)
+        pl.semaphore_signal(barrier, inc=1, device_id=partner, device_id_type=MESH)
+        for d in range(1, group):
+            pl.semaphore_signal(barrier, inc=1, device_id=member(d), device_id_type=MESH)
+        others = group + (1 - core) * ((r + rows - 1) // rows) + core * ((2 * rows - 2 - r) // rows)
+    else:
+        greet_left, greet_right = has_left, has_right
+        pl.semaphore_signal(barrier, inc=1, device_id=(up, r), device_id_type=MESH)
+        pl.semaphore_signal(barrier, inc=1, device_id=(down, r), device_id_type=MESH)
+        others = 2 + (r + rows - 1) // rows + (2 * rows - 2 - r) // rows
+
+    @pl.when(greet_left)
     def _():
         pl.semaphore_signal(barrier, inc=1, device_id=(s, r - 1), device_id_type=MESH)
 
-    @pl.when(has_right)
+    @pl.when(greet_right)
     def _():
         pl.semaphore_signal(barrier, inc=1, device_id=(s, r + 1), device_id_type=MESH)
+
+    if fused:
+        local, folded, parts, total_sum, pair_send, pair_recv, a_send, a_recv, b_send, b_recv = sum_refs
+        half = vectors // 2
+        chunk = half // group
+        mine = pl.ds(pl.multiple_of(core * half, half), half)
+        theirs = pl.ds(pl.multiple_of((1 - core) * half, half), half)
+        spot = pl.ds(pl.multiple_of(core * half + me * chunk, chunk), chunk)
+
+        def swap_copy(m):
+            return pltpu.make_async_remote_copy(
+                src_ref=local.at[m, theirs], dst_ref=folded.at[m],
+                send_sem=pair_send.at[m, 0], recv_sem=pair_recv.at[m, 0],
+                device_id=partner, device_id_type=MESH,
+            )
+
+        def join_copy(m):
+            return pltpu.make_async_remote_copy(
+                src_ref=total_sum.at[m, mine], dst_ref=total_sum.at[m, mine],
+                send_sem=pair_send.at[m, 1], recv_sem=pair_recv.at[m, 1],
+                device_id=partner, device_id_type=MESH,
+            )
+
+        def scatter_copy(m, d):
+            q = lax.rem(me + d, group)
+            return pltpu.make_async_remote_copy(
+                src_ref=folded.at[m, pl.ds(pl.multiple_of(q * chunk, chunk), chunk)], dst_ref=parts.at[m, d],
+                send_sem=a_send.at[m, d], recv_sem=a_recv.at[m, d], device_id=member(d), device_id_type=MESH,
+            )
+
+        def spread_copy(m, d):
+            return pltpu.make_async_remote_copy(
+                src_ref=total_sum.at[m, spot], dst_ref=total_sum.at[m, spot],
+                send_sem=b_send.at[m, d], recv_sem=b_recv.at[m, d], device_id=member(d), device_id_type=MESH,
+            )
+
+        def sum_begin(m, gram):
+            local[m] = gram
+            swap_copy(m).start()
+
+        def sum_scatter(m):
+            swap_copy(m).wait()
+            folded[m] += local[m, mine]
+            for d in range(1, group):
+                scatter_copy(m, d).start()
+
+        def sum_spread(m):
+            acc = folded[m, pl.ds(pl.multiple_of(me * chunk, chunk), chunk)]
+            for d in range(1, group):
+                scatter_copy(m, d).wait()
+                acc += parts[m, d]
+            total_sum[m, spot] = acc
+            for d in range(1, group):
+                spread_copy(m, d).start()
+
+        def sum_join(m):
+            for d in range(1, group):
+                spread_copy(m, d).wait()
+            join_copy(m).start()
+
+        def sum_end(m):
+            join_copy(m).wait()
+            gram_ref[m * vectors:(m + 1) * vectors] = total_sum[m]
 
     def slab_copies(t):
         p, h = (t // halves) % 2, t % halves
@@ -168,124 +252,49 @@
         for c in range(cols):
             ext[0][h][first + c] = panel_ref[c, :, h * lanes:(h + 1) * lanes]
 
-    pl.semaphore_wait(barrier, 2 + (r + rows - 1) // rows + (2 * rows - 2 - r) // rows)
+    pl.semaphore_wait(barrier, others)
 
     for h in range(halves):
         start_slab(h)
     y_ref[...] = panel_ref[...].astype(jnp.float32)
     total = halves * (DEG + 1)
-    vectors = y_ref.shape[-1]
     depth = cols * y_ref.shape[1]
+    last = halves * DEG
     for t in range(total + 1):
+        if fused and t == last + 2:
+            sum_spread(0)
         if t >= 1:
             wait_row(t - 1)
             compute(t - 1)
             if halves <= t - 1 + halves < total:
                 start_slab(t - 1 + halves)
-            if t - 1 == halves * DEG - 1:
+            if t == last:
                 flat = y_ref[...].reshape(depth, vectors)
                 weight = mass_ref[...].reshape(depth, lanes)
                 weighted = jnp.concatenate([weight] * halves, axis=1) * flat
-                gram_ref[:vectors] = split3_dot(weighted, flat, ((0,), (0,)))
+                gram = split3_dot(weighted, flat, ((0,), (0,)))
+                if fused:
+                    sum_begin(0, gram)
+                else:
+                    gram_ref[:vectors] = gram
+            if fused and t == last + 1:
+                sum_scatter(0)
         if t < total:
             wait_slab(t)
             start_row(t)
-    gram_ref[vectors:] = split3_dot(
+    gram = split3_dot(
         y_ref[...].reshape(depth, vectors), ky_ref[...].reshape(depth, vectors), ((0,), (0,))
     )
-
-
-def sum_kernel(slabs, rows, g_ref, out_ref, first, parts, total, pair_send, pair_recv, a_send, a_recv, b_send, b_recv):
-    half = g_ref.shape[0] // 2
-    group = slabs * (rows // 2)
-    chunk = half // group
-    s = lax.axis_index("slab")
-    r = lax.axis_index("row")
-    core = lax.rem(r, 2)
-    me = s * (rows // 2) + r // 2
-    partner = (s, r + 1 - 2 * core)
-
-    def member(d):
-        q = lax.rem(me + d, group)
-        return (q // (rows // 2), lax.rem(q, rows // 2) * 2 + core)
-
-    barrier = pltpu.get_barrier_semaphore()
-    pl.semaphore_signal(barrier, inc=1, device_id=partner, device_id_type=MESH)
-    for d in range(1, group):
-        pl.semaphore_signal(barrier, inc=1, device_id=member(d), device_id_type=MESH)
-    pl.semaphore_wait(barrier, group)
-
-    mine = pl.ds(pl.multiple_of(core * half, half), half)
-    theirs = pl.ds(pl.multiple_of((1 - core) * half, half), half)
-    swap = pltpu.make_async_remote_copy(
-        src_ref=g_ref.at[theirs], dst_ref=first, send_sem=pair_send.at[0], recv_sem=pair_recv.at[0],
-        device_id=partner, device_id_type=MESH,
-    )
-    swap.start()
-    swap.wait()
-    first[...] += g_ref[mine]
-    copies = []
-    for d in range(1, group):
-        q = lax.rem(me + d, group)
-        copy = pltpu.make_async_remote_copy(
-            src_ref=first.at[pl.ds(pl.multiple_of(q * chunk, chunk), chunk)], dst_ref=parts.at[d],
-            send_sem=a_send.at[d], recv_sem=a_recv.at[d], device_id=member(d), device_id_type=MESH,
-        )
-        copy.start()
-        copies.append(copy)
-    acc = first[pl.ds(pl.multiple_of(me * chunk, chunk), chunk)]
-    for d, copy in enumerate(copies, 1):
-        copy.wait()
-        acc += parts[d]
-    spot = pl.ds(pl.multiple_of(core * half + me * chunk, chunk), chunk)
-    total[spot] = acc
-    copies = []
-    for d in range(1, group):
-        copy = pltpu.make_async_remote_copy(
-            src_ref=total.at[spot], dst_ref=total.at[spot],
-            send_sem=b_send.at[d], recv_sem=b_recv.at[d], device_id=member(d), device_id_type=MESH,
-        )
-        copy.start()
-        copies.append(copy)
-    for copy in copies:
-        copy.wait()
-    swap = pltpu.make_async_remote_copy(
-        src_ref=total.at[mine], dst_ref=total.at[mine], send_sem=pair_send.at[1], recv_sem=pair_recv.at[1],
-        device_id=partner, device_id_type=MESH,
-    )
-    swap.start()
-    swap.wait()
-    out_ref[...] = total[...]
-
-
-def sum_everywhere(grams, slabs, rows):
-    height, width = grams.shape
-    group = slabs * rows // 2
-    if rows % 2 or height % (2 * group) or (height // (2 * group)) % 8:
-        return lax.psum(grams, ("slab", "row"))
-    half = height // 2
-    vmem = pl.BlockSpec(memory_space=pltpu.VMEM)
-    return pl.pallas_call(
-        functools.partial(sum_kernel, slabs, rows),
-        out_shape=jax.ShapeDtypeStruct(grams.shape, jnp.float32),
-        in_specs=[vmem],
-        out_specs=vmem,
-        scratch_shapes=[
-            pltpu.VMEM((half, width), jnp.float32),
-            pltpu.VMEM((group, half // group, width), jnp.float32),
-            pltpu.VMEM((height, width), jnp.float32),
-            pltpu.SemaphoreType.DMA((2,)),
-            pltpu.SemaphoreType.DMA((2,)),
-            pltpu.SemaphoreType.DMA((group,)),
-            pltpu.SemaphoreType.DMA((group,)),
-            pltpu.SemaphoreType.DMA((group,)),
-            pltpu.SemaphoreType.DMA((group,)),
-        ],
-        compiler_params=pltpu.CompilerParams(
-            collective_id=1, has_side_effects=True, vmem_limit_bytes=16 * 1024 * 1024
-        ),
-        name="sum_everywhere",
-    )(grams)
+    if fused:
+        sum_begin(1, gram)
+        sum_join(0)
+        sum_scatter(1)
+        sum_end(0)
+        sum_spread(1)
+        sum_join(1)
+        sum_end(1)
+    else:
+        gram_ref[vectors:] = gram
 
 
 def ritz_kernel(total_rows, gram_ref, y_ref, ky_ref, basis_ref, matrix_ref, image_ref, scaled, resid, factor):
@@ -365,8 +374,19 @@
     vmem = pl.BlockSpec(memory_space=pltpu.VMEM)
     field = jax.ShapeDtypeStruct((cols, block_rows, vectors), jnp.float32)
     cells = 3 * (cols + 2)
+    group = slabs * (rows // 2)
+    half = vectors // 2
+    fused = halves == 2 and rows % 2 == 0 and half % group == 0 and (half // group) % 8 == 0
+    sum_scratch = [
+        pltpu.VMEM((2, vectors, vectors), jnp.float32),
+        pltpu.VMEM((2, half, vectors), jnp.float32),
+        pltpu.VMEM((2, group, half // group, vectors), jnp.float32),
+        pltpu.VMEM((2, vectors, vectors), jnp.float32),
+        pltpu.SemaphoreType.DMA((2, 2)),
+        pltpu.SemaphoreType.DMA((2, 2)),
+    ] + [pltpu.SemaphoreType.DMA((2, group))] * 4
     y, ky, grams = pl.pallas_call(
-        functools.partial(filter_kernel, slabs, rows, cols, slots, halves, lanes),
+        functools.partial(filter_kernel, slabs, rows, cols, slots, halves, lanes, fused),
         out_shape=(field, field, jax.ShapeDtypeStruct((2 * vectors, vectors), jnp.float32)),
         in_specs=[pl.BlockSpec(memory_space=pltpu.SMEM)] + [vmem] * 5,
         out_specs=(vmem, vmem, vmem),
@@ -377,13 +397,15 @@
             pltpu.SemaphoreType.DMA((2, halves, 2)),
             pltpu.SemaphoreType.DMA((2, halves, 2, 3)),
             pltpu.SemaphoreType.DMA((2, halves, 2, 3)),
-        ],
+        ]
+        + (sum_scratch if fused else []),
         compiler_params=pltpu.CompilerParams(
             collective_id=0, has_side_effects=True, vmem_limit_bytes=32 * 1024 * 1024
         ),
         name="filter_and_grams",
     )(neighbour_index(offsets, cols), panel[0], blocks[0], spread(1.0 / mass), spread(stiff_diag[0]), spread(mass))
-    grams = sum_everywhere(grams, slabs, rows)
+    if not fused:
+        grams = lax.psum(grams, ("slab", "row"))
     square = jax.ShapeDtypeStruct((vectors, vectors), jnp.float32)
     ritz_basis, ritz_matrix, stiff_image = pl.pallas_call(
         functools.partial(ritz_kernel, total_rows),

time: 196 us -> 196 us (level)
    pallas_call x1 -> x0, Pallas kernels: 27.1 us -> none  [sum_everywhere(): pl.pallas_call(functools.partial(sum_kernel, slabs, rows), out_shape=jax....]
    pallas_call x1, Pallas kernels: 121 us -> 148 us  [shards(): pl.pallas_call(functools.partial(filter_kernel, slabs, rows, cols, slots,...]
where the time goes in v3:
time: 196 us; the launch traced here: 195 us
  Pallas kernels  191 us (97%)
  local copies, waits for them, and re-layouts  2.12 us (1%)
    pallas_call x1, Pallas kernels, shards(): pl.pallas_call(functools.partial(filter_kernel, slabs, rows, cols, slots,...  148 us
    pallas_call x1, Pallas kernels, shards(): pl.pallas_call(functools.partial(ritz_kernel, total_rows), out_shape=(fie...  43.1 us

profile of v3, /device:TPU:0, one launch (start us, length us, event | category | flops | bytes accessed | tf_op | source)
XLA Modules:
  0.0 195.3 jit_solution(13099484617259957059)
XLA Ops:
  0.6 0.0 copy-start
  0.6 0.0 copy-start.1
  0.7 0.8 fusion.2
  1.4 0.1 reshape.36.index_ref
  1.5 0.0 copy-done
  1.5 0.9 broadcast_divide_fusion
  2.4 0.1 broadcast_in_dim.12.inv_ref
  2.5 0.1 broadcast_in_dim.30.mass_ref
  2.7 0.8 broadcast_in_dim.14.diag_ref
  3.5 0.0 copy-done.1
  3.5 0.0 copy-start.2
  3.5 0.9 copy-done.2
  4.5 147.7 %filter_and_grams.1 = (f32[4,128,256]{2,1,0:T(8,128)S(1)}, f32[4,128,256]{2,1,0:T(8,128)S(1)}, f32[512,256]{1,0:T(8,128)S(1)}) custom-call(s32[24]{0:T(128)S(1)} %reshape.36.index_ref, bf16[4,128,256]{2,1,0:T(8,128)(2,1)S(1)} %bitcast.16, bf16[4,6,128,128]{3,2,1,0:T(8,128)(2,1)S(1)} %bitcast.15, f32[4,128,128]{2,1,0:T(8,128)S(1)} %broadcast_in_dim.12.inv_ref, ...), custom_call_target="tpu_custom_call" | custom-call | tf_op jit(solution)/shard_map/filter_and_grams/pallas_call | solution.py:388
  152.2 43.1 %ritz.1 = (f32[4,128,256]{2,1,0:T(8,128)}, f32[256,256]{1,0:T(8,128)}, f32[4,128,256]{2,1,0:T(8,128)}) custom-call(f32[512,256]{1,0:T(8,128)S(1)} %get-tuple-element.9.gram_ref, f32[4,128,256]{2,1,0:T(8,128)S(1)} %get-tuple-element.10.y_ref, f32[4,128,256]{2,1,0:T(8,128)S(1)} %get-tuple-element.11.ky_ref), custom_call_target="tpu_custom_call" | custom-call | tf_op jit(solution)/shard_map/ritz/pallas_call | solution.py:410
Async XLA Ops:
  0.6 0.9 copy-start
  0.6 2.9 %copy-start.1 = (bf16[1,4,6,128,128]{4,3,2,1,0:T(8,128)(2,1)S(1)}, bf16[1,4,6,128,128]{4,3,2,1,0:T(8,128)(2,1)}, u32[]{:S(2)}) copy-start(bf16[1,4,6,128,128]{4,3,2,1,0:T(8,128)(2,1)} %param.8) | copy-start | bytes 2359300
  3.5 1.0 copy-start.2

commit v4 on v3

--- a/solution.py
+++ b/solution.py
@@ -188,17 +188,19 @@
     def start_slab(t):
         for copy in slab_copies(t):
             copy.start()
+        start_row(t, (1,))
 
     def wait_slab(t):
         for copy in slab_copies(t):
             copy.wait()
 
-    def start_row(t):
+    def start_row(t, which):
         for side, there in ((0, has_right), (1, has_left)):
             @pl.when(there)
             def _():
-                for copy in row_copies(t, side):
-                    copy.start()
+                copies = row_copies(t, side)
+                for k in which:
+                    copies[k].start()
 
     def wait_row(t):
         for side, there in ((0, has_right), (1, has_left)):
@@ -261,8 +263,6 @@
     depth = cols * y_ref.shape[1]
     last = halves * DEG
     for t in range(total + 1):
-        if fused and t == last + 2:
-            sum_spread(0)
         if t >= 1:
             wait_row(t - 1)
             compute(t - 1)
@@ -281,17 +281,18 @@
                 sum_scatter(0)
         if t < total:
             wait_slab(t)
-            start_row(t)
+            start_row(t, (0, 2))
     gram = split3_dot(
         y_ref[...].reshape(depth, vectors), ky_ref[...].reshape(depth, vectors), ((0,), (0,))
     )
     if fused:
         sum_begin(1, gram)
+        sum_spread(0)
+        sum_scatter(1)
         sum_join(0)
-        sum_scatter(1)
-        sum_end(0)
         sum_spread(1)
         sum_join(1)
+        sum_end(0)
         sum_end(1)
     else:
         gram_ref[vectors:] = gram

time: 196 us -> 196 us (level)
  no operation moved by 1% of the time
where the time goes in v4:
time: 196 us; the launch traced here: 195 us
  Pallas kernels  191 us (97%)
  local copies, waits for them, and re-layouts  2.12 us (1%)
    pallas_call x1, Pallas kernels, shards(): pl.pallas_call(functools.partial(filter_kernel, slabs, rows, cols, slots,...  148 us
    pallas_call x1, Pallas kernels, shards(): pl.pallas_call(functools.partial(ritz_kernel, total_rows), out_shape=(fie...  43.1 us

profile of v4, /device:TPU:0, one launch (start us, length us, event | category | flops | bytes accessed | tf_op | source)
XLA Modules:
  0.0 195.4 jit_solution(10530630561926715196)
XLA Ops:
  0.6 0.0 copy-start
  0.6 0.0 copy-start.1
  0.7 0.8 fusion.2
  1.4 0.1 reshape.36.index_ref
  1.5 0.0 copy-done
  1.5 0.9 broadcast_divide_fusion
  2.4 0.1 broadcast_in_dim.12.inv_ref
  2.5 0.1 broadcast_in_dim.30.mass_ref
  2.7 0.8 broadcast_in_dim.14.diag_ref
  3.5 0.0 copy-done.1
  3.5 0.0 copy-start.2
  3.5 0.9 copy-done.2
  4.5 147.8 %filter_and_grams.1 = (f32[4,128,256]{2,1,0:T(8,128)S(1)}, f32[4,128,256]{2,1,0:T(8,128)S(1)}, f32[512,256]{1,0:T(8,128)S(1)}) custom-call(s32[24]{0:T(128)S(1)} %reshape.36.index_ref, bf16[4,128,256]{2,1,0:T(8,128)(2,1)S(1)} %bitcast.16, bf16[4,6,128,128]{3,2,1,0:T(8,128)(2,1)S(1)} %bitcast.15, f32[4,128,128]{2,1,0:T(8,128)S(1)} %broadcast_in_dim.12.inv_ref, ...), custom_call_target="tpu_custom_call" | custom-call | tf_op jit(solution)/shard_map/filter_and_grams/pallas_call | solution.py:389
  152.3 43.1 %ritz.1 = (f32[4,128,256]{2,1,0:T(8,128)}, f32[256,256]{1,0:T(8,128)}, f32[4,128,256]{2,1,0:T(8,128)}) custom-call(f32[512,256]{1,0:T(8,128)S(1)} %get-tuple-element.9.gram_ref, f32[4,128,256]{2,1,0:T(8,128)S(1)} %get-tuple-element.10.y_ref, f32[4,128,256]{2,1,0:T(8,128)S(1)} %get-tuple-element.11.ky_ref), custom_call_target="tpu_custom_call" | custom-call | tf_op jit(solution)/shard_map/ritz/pallas_call | solution.py:411
Async XLA Ops:
  0.6 0.9 copy-start
  0.6 2.9 %copy-start.1 = (bf16[1,4,6,128,128]{4,3,2,1,0:T(8,128)(2,1)S(1)}, bf16[1,4,6,128,128]{4,3,2,1,0:T(8,128)(2,1)}, u32[]{:S(2)}) copy-start(bf16[1,4,6,128,128]{4,3,2,1,0:T(8,128)(2,1)} %param.8) | copy-start | bytes 2359300
  3.5 1.0 copy-start.2

commit v5 on v4

--- a/solution.py
+++ b/solution.py
@@ -175,7 +175,7 @@
     def row_copies(t, side):
         p, h = (t // halves) % 2, t % halves
         buf = ext[p][h]
-        source, place, target = ((cols, 0, r + 1), (1, cols + 1, r - 1))[side]
+        source, place, target = ((cols, 0, lax.rem(r + 1, rows)), (1, cols + 1, lax.rem(r + rows - 1, rows)))[side]
         return [
             pltpu.make_async_remote_copy(
                 src_ref=buf.at[pl.ds(source + wide * k, 1)], dst_ref=buf.at[pl.ds(place + wide * k, 1)],

time: 196 us -> 196 us (level)
  no operation moved by 1% of the time
where the time goes in v5:
time: 196 us; the launch traced here: 195 us
  Pallas kernels  191 us (97%)
  local copies, waits for them, and re-layouts  2.12 us (1%)
    pallas_call x1, Pallas kernels, shards(): pl.pallas_call(functools.partial(filter_kernel, slabs, rows, cols, slots,...  148 us
    pallas_call x1, Pallas kernels, shards(): pl.pallas_call(functools.partial(ritz_kernel, total_rows), out_shape=(fie...  43.1 us

profile of v5, /device:TPU:0, one launch (start us, length us, event | category | flops | bytes accessed | tf_op | source)
XLA Modules:
  0.0 195.4 jit_solution(4638096633604995867)
XLA Ops:
  0.6 0.0 copy-start
  0.6 0.0 copy-start.1
  0.7 0.8 fusion.2
  1.4 0.1 reshape.36.index_ref
  1.5 0.0 copy-done
  1.5 0.9 broadcast_divide_fusion
  2.4 0.1 broadcast_in_dim.12.inv_ref
  2.5 0.1 broadcast_in_dim.30.mass_ref
  2.7 0.8 broadcast_in_dim.14.diag_ref
  3.5 0.0 copy-done.1
  3.5 0.0 copy-start.2
  3.5 0.9 copy-done.2
  4.5 147.8 %filter_and_grams.1 = (f32[4,128,256]{2,1,0:T(8,128)S(1)}, f32[4,128,256]{2,1,0:T(8,128)S(1)}, f32[512,256]{1,0:T(8,128)S(1)}) custom-call(s32[24]{0:T(128)S(1)} %reshape.36.index_ref, bf16[4,128,256]{2,1,0:T(8,128)(2,1)S(1)} %bitcast.16, bf16[4,6,128,128]{3,2,1,0:T(8,128)(2,1)S(1)} %bitcast.15, f32[4,128,128]{2,1,0:T(8,128)S(1)} %broadcast_in_dim.12.inv_ref, ...), custom_call_target="tpu_custom_call" | custom-call | tf_op jit(solution)/shard_map/filter_and_grams/pallas_call | solution.py:389
  152.3 43.1 %ritz.1 = (f32[4,128,256]{2,1,0:T(8,128)}, f32[256,256]{1,0:T(8,128)}, f32[4,128,256]{2,1,0:T(8,128)}) custom-call(f32[512,256]{1,0:T(8,128)S(1)} %get-tuple-element.9.gram_ref, f32[4,128,256]{2,1,0:T(8,128)S(1)} %get-tuple-element.10.y_ref, f32[4,128,256]{2,1,0:T(8,128)S(1)} %get-tuple-element.11.ky_ref), custom_call_target="tpu_custom_call" | custom-call | tf_op jit(solution)/shard_map/ritz/pallas_call | solution.py:411
Async XLA Ops:
  0.6 0.9 copy-start
  0.6 2.9 %copy-start.1 = (bf16[1,4,6,128,128]{4,3,2,1,0:T(8,128)(2,1)S(1)}, bf16[1,4,6,128,128]{4,3,2,1,0:T(8,128)(2,1)}, u32[]{:S(2)}) copy-start(bf16[1,4,6,128,128]{4,3,2,1,0:T(8,128)(2,1)} %param.8) | copy-start | bytes 2359300
  3.5 1.0 copy-start.2
